TPU v7x, 32 devices: a whole 2x2x4 slice. The times are simulated.
32 devices in a mesh: dp: 4 (over y, x), fsdp: 8 (over z, core).
Axes of the slice: x: 2, y: 2, z: 4, core: 2. Of those that a mesh axis runs over, the one named last changes fastest.
Arguments:
- layer_input: bfloat16 [32, 1024, 768], P(('dp', 'fsdp')), may hold values from -6 to 6
- lengths: int32 [32], P(('dp', 'fsdp')), may hold values from 64 to 1024, as said below
- ln1_gain: bfloat16 [768], P(('dp', 'fsdp')), may hold values from 0.099609375 to 1.8984375
- ln1_bias: bfloat16 [768], P(('dp', 'fsdp')), may hold values from -3 to 3
- w_qkv: bfloat16 [768, 2304], P(('dp', 'fsdp')), may hold values from -0.3125 to 0.3125
- b_qkv: bfloat16 [2304], P(('dp', 'fsdp')), may hold values from -3 to 3
- w_out: bfloat16 [768, 768], P(('dp', 'fsdp')), may hold values from -1.25 to 1.25
- b_out: bfloat16 [768], P(('dp', 'fsdp')), may hold values from -2 to 2
- ln2_gain: bfloat16 [768], P(('dp', 'fsdp')), may hold values from 0.099609375 to 1.8984375
- ln2_bias: bfloat16 [768], P(('dp', 'fsdp')), may hold values from -3 to 3
- w_up: bfloat16 [768, 3072], P(('dp', 'fsdp')), may hold values from -0.21875 to 0.21875
- b_up: bfloat16 [3072], P(('dp', 'fsdp')), may hold values from -3 to 3
- w_down: bfloat16 [3072, 768], P(('dp', 'fsdp')), may hold values from -0.109375 to 0.109375
- b_down: bfloat16 [768], P(('dp', 'fsdp')), may hold values from -2 to 2
- cotangent: bfloat16 [32, 1024, 768], P(('dp', 'fsdp')), may hold values from -6 to 6
Outputs:
- result: bfloat16 [32, 1024, 768], P(('dp', 'fsdp'))
- grad_input: float32 [32, 1024, 768], P(('dp', 'fsdp'))
- grad_ln1_gain: float32 [768], P(('dp', 'fsdp'))
- grad_ln1_bias: float32 [768], P(('dp', 'fsdp'))
- grad_w_qkv: float32 [768, 2304], P(('dp', 'fsdp'))
- grad_b_qkv: float32 [2304], P(('dp', 'fsdp'))
- grad_w_out: float32 [768, 768], P(('dp', 'fsdp'))
- grad_b_out: float32 [768], P(('dp', 'fsdp'))
- grad_ln2_gain: float32 [768], P(('dp', 'fsdp'))
- grad_ln2_bias: float32 [768], P(('dp', 'fsdp'))
- grad_w_up: float32 [768, 3072], P(('dp', 'fsdp'))
- grad_b_up: float32 [3072], P(('dp', 'fsdp'))
- grad_w_down: float32 [3072, 768], P(('dp', 'fsdp'))
- grad_b_down: float32 [768], P(('dp', 'fsdp'))
Inputs may be any that keep to these rules, and one draw needn't show every extreme that they name: `lengths`: some slot has length exactly 1024.
All inputs are finite; a program needn't handle non-finite values.
Results may differ from a plain program's by a relative error of at most 0.012.
The roundings to bfloat16 on the way count: a program that leaves them out, or rounds other values in their place, can miss the bound.
Values may be sent and summed in bfloat16 or wider, within the bound.
No kernel may reach another device: no remote copies, remote signals or barrier semaphores. Data moves between devices by JAX's collectives and lax.ppermute only.
A program may use at most 192 MiB of HBM per device.

v0:
```python
import jax
import jax.numpy as jnp
from jax import lax
from jax.sharding import PartitionSpec as P

H = 12
HD = 64


norm_eps = 1e-05


def norm_forward(values, gain, bias):
    mean = jnp.mean(values, axis=-1, keepdims=True)
    centred = values - mean
    inverse = lax.rsqrt(jnp.mean(centred * centred, axis=-1, keepdims=True) + norm_eps)
    normal = centred * inverse
    return (normal * gain + bias, normal, inverse)


def norm_backward(grad_in, normal, inverse, gain):
    grad_normal = grad_in * gain
    inner = (
        grad_normal
        - jnp.mean(grad_normal, axis=-1, keepdims=True)
        - normal * jnp.mean(grad_normal * normal, axis=-1, keepdims=True)
    )
    return (inner * inverse, jnp.sum(grad_in * normal, axis=0), jnp.sum(grad_in, axis=0))


def gelu_tanh(values):
    return jax.nn.gelu(values, approximate=True)


def gelu_grad(hidden, grad_in):
    unused, pullback = jax.vjp(gelu_tanh, hidden)
    return pullback(grad_in)[0]


def head_forward(queries, keys_in, values, allowed, scale):
    scores = (
        jnp.einsum("gqd,gkd->gqk", queries, keys_in, preferred_element_type=jnp.float32) * scale
    )
    magnitude = jnp.sqrt(scores * scores + 1.0)
    row_top = jnp.max(jnp.where(allowed, magnitude, 0.0), axis=-1, keepdims=True)
    exp_terms = jnp.where(allowed, jnp.exp(magnitude - row_top), 0.0)
    row_total = jnp.sum(exp_terms, axis=-1, keepdims=True)
    weighted = (scores / magnitude * (exp_terms / row_total)).astype(jnp.bfloat16)
    mixed = jnp.einsum("gqk,gkd->gqd", weighted, values, preferred_element_type=jnp.float32)
    return (mixed, (row_top + jnp.log(row_total))[..., 0])


def head_backward(queries, keys_in, values, grad_mixed, log_total, allowed, scale):
    scores = (
        jnp.einsum("gqd,gkd->gqk", queries, keys_in, preferred_element_type=jnp.float32) * scale
    )
    magnitude = jnp.sqrt(scores * scores + 1.0)
    share = jnp.where(allowed, jnp.exp(magnitude - log_total[..., None]), 0.0)
    ratio = scores / magnitude
    weights = ratio * share
    grad_values = jnp.einsum(
        "gqk,gqd->gkd", weights.astype(jnp.bfloat16), grad_mixed, preferred_element_type=jnp.float32
    )
    grad_weights = jnp.einsum(
        "gqd,gkd->gqk", grad_mixed, values, preferred_element_type=jnp.float32
    )
    along = jnp.sum(grad_weights * weights, axis=-1, keepdims=True)
    grad_scores = grad_weights * share / (magnitude * magnitude * magnitude) + ratio * (
        grad_weights * weights - share * along
    )
    grad_low = grad_scores.astype(jnp.bfloat16)
    grad_queries = (
        jnp.einsum("gqk,gkd->gqd", grad_low, keys_in, preferred_element_type=jnp.float32) * scale
    )
    grad_keys = (
        jnp.einsum("gqk,gqd->gkd", grad_low, queries, preferred_element_type=jnp.float32) * scale
    )
    return (grad_queries, grad_keys, grad_values)


def body(
    layer_input,
    lengths,
    ln1_gain,
    ln1_bias,
    w_qkv,
    b_qkv,
    w_out,
    b_out,
    ln2_gain,
    ln2_bias,
    w_up,
    b_up,
    w_down,
    b_down,
    cotangent,
):
    seq_count, slot_len, width = layer_input.shape
    rows = seq_count * slot_len
    scale = HD ** (-0.5)
    position = jnp.arange(slot_len, dtype=jnp.int32)
    live_rows = position[None, :] < lengths[:, None]
    allowed = (position[None, :, None] >= position[None, None, :]) & live_rows[:, None, :]
    live_flat = live_rows.reshape(rows, 1)
    full_qkv, bias_qkv, full_out, bias_out, gain_low_one, shift_one = (
        lax.all_gather(w_qkv, ("dp", "fsdp"), axis=0, tiled=True),
        lax.all_gather(b_qkv, ("dp", "fsdp"), axis=0, tiled=True),
        lax.all_gather(w_out, ("dp", "fsdp"), axis=0, tiled=True),
        lax.all_gather(b_out, ("dp", "fsdp"), axis=0, tiled=True),
        lax.all_gather(ln1_gain, ("dp", "fsdp"), axis=0, tiled=True),
        lax.all_gather(ln1_bias, ("dp", "fsdp"), axis=0, tiled=True),
    )
    gain_one = gain_low_one.astype(jnp.float32)
    inputs = layer_input.reshape(rows, width).astype(jnp.float32)
    first, first_normal, first_inverse = norm_forward(
        inputs, gain_one, shift_one.astype(jnp.float32)
    )
    first_low = first.astype(jnp.bfloat16)
    projected = (
        jnp.dot(first_low, full_qkv, preferred_element_type=jnp.float32)
        + bias_qkv.astype(jnp.float32)
    ).astype(jnp.bfloat16)
    pieces = projected.reshape(seq_count, slot_len, 3, H, HD).transpose(2, 3, 0, 1, 4)

    def forward_head(head_in):
        return head_forward(head_in[0], head_in[1], head_in[2], allowed, scale)

    head_out, log_total = lax.map(forward_head, (pieces[0], pieces[1], pieces[2]))
    mixed_low = head_out.transpose(1, 2, 0, 3).reshape(rows, width).astype(jnp.bfloat16)
    attended = jnp.dot(mixed_low, full_out, preferred_element_type=jnp.float32) + bias_out.astype(
        jnp.float32
    )
    residual = inputs + attended
    full_up, bias_up, full_down, bias_down, gain_low_two, shift_two = (
        lax.all_gather(w_up, ("dp", "fsdp"), axis=0, tiled=True),
        lax.all_gather(b_up, ("dp", "fsdp"), axis=0, tiled=True),
        lax.all_gather(w_down, ("dp", "fsdp"), axis=0, tiled=True),
        lax.all_gather(b_down, ("dp", "fsdp"), axis=0, tiled=True),
        lax.all_gather(ln2_gain, ("dp", "fsdp"), axis=0, tiled=True),
        lax.all_gather(ln2_bias, ("dp", "fsdp"), axis=0, tiled=True),
    )
    gain_two = gain_low_two.astype(jnp.float32)
    second, second_normal, second_inverse = norm_forward(
        residual, gain_two, shift_two.astype(jnp.float32)
    )
    second_low = second.astype(jnp.bfloat16)
    hidden = jnp.dot(second_low, full_up, preferred_element_type=jnp.float32) + bias_up.astype(
        jnp.float32
    )
    activated = gelu_tanh(hidden).astype(jnp.bfloat16)
    branch = jnp.dot(activated, full_down, preferred_element_type=jnp.float32) + bias_down.astype(
        jnp.float32
    )
    result = (
        jnp.where(live_flat, residual + branch, 0.0).astype(jnp.bfloat16).reshape(layer_input.shape)
    )
    grad_out = jnp.where(live_flat, cotangent.reshape(rows, width).astype(jnp.float32), 0.0)
    grad_branch = grad_out.astype(jnp.bfloat16)
    full_up, full_down, gain_back_two = (
        lax.all_gather(w_up, ("dp", "fsdp"), axis=0, tiled=True),
        lax.all_gather(w_down, ("dp", "fsdp"), axis=0, tiled=True),
        lax.all_gather(ln2_gain, ("dp", "fsdp"), axis=0, tiled=True),
    )
    gain_two = gain_back_two.astype(jnp.float32)
    grad_wdown = jnp.einsum("rf,rd->fd", activated, grad_branch, preferred_element_type=jnp.float32)
    grad_bdown = jnp.sum(grad_branch.astype(jnp.float32), axis=0)
    grad_act = jnp.einsum("rd,fd->rf", grad_branch, full_down, preferred_element_type=jnp.float32)
    grad_hidden = gelu_grad(hidden, grad_act).astype(jnp.bfloat16)
    grad_wup = jnp.einsum("rd,rf->df", second_low, grad_hidden, preferred_element_type=jnp.float32)
    grad_bup = jnp.sum(grad_hidden.astype(jnp.float32), axis=0)
    grad_second = jnp.einsum("rf,df->rd", grad_hidden, full_up, preferred_element_type=jnp.float32)
    grad_norm_two, grad_gain_two, grad_shift_two = norm_backward(
        grad_second, second_normal, second_inverse, gain_two
    )
    grad_resid = grad_out + grad_norm_two
    grad_attn = grad_resid.astype(jnp.bfloat16)
    full_qkv, full_out, gain_back_one = (
        lax.all_gather(w_qkv, ("dp", "fsdp"), axis=0, tiled=True),
        lax.all_gather(w_out, ("dp", "fsdp"), axis=0, tiled=True),
        lax.all_gather(ln1_gain, ("dp", "fsdp"), axis=0, tiled=True),
    )
    gain_one = gain_back_one.astype(jnp.float32)
    grad_wout = jnp.einsum("rd,re->de", mixed_low, grad_attn, preferred_element_type=jnp.float32)
    grad_bout = jnp.sum(grad_attn.astype(jnp.float32), axis=0)
    grad_mixed = jnp.einsum(
        "re,de->rd", grad_attn, full_out, preferred_element_type=jnp.float32
    ).astype(jnp.bfloat16)
    grad_heads = grad_mixed.reshape(seq_count, slot_len, H, HD).transpose(2, 0, 1, 3)

    def backward_head(head_in):
        return head_backward(
            head_in[0], head_in[1], head_in[2], head_in[3], head_in[4], allowed, scale
        )

    grad_queries, grad_keys, grad_values = lax.map(
        backward_head, (pieces[0], pieces[1], pieces[2], grad_heads, log_total)
    )
    grad_proj = (
        jnp.stack((grad_queries, grad_keys, grad_values))
        .transpose(2, 3, 0, 1, 4)
        .reshape(rows, 3 * width)
        .astype(jnp.bfloat16)
    )
    grad_wqkv = jnp.einsum("rd,re->de", first_low, grad_proj, preferred_element_type=jnp.float32)
    grad_bqkv = jnp.sum(grad_proj.astype(jnp.float32), axis=0)
    grad_first = jnp.einsum("re,de->rd", grad_proj, full_qkv, preferred_element_type=jnp.float32)
    grad_norm_one, grad_gain_one, grad_shift_one = norm_backward(
        grad_first, first_normal, first_inverse, gain_one
    )
    grad_inputs = (grad_resid + grad_norm_one).reshape(layer_input.shape)
    shards = (
        lax.psum_scatter(grad_gain_one, ("dp", "fsdp"), scatter_dimension=0, tiled=True),
        lax.psum_scatter(grad_shift_one, ("dp", "fsdp"), scatter_dimension=0, tiled=True),
        lax.psum_scatter(grad_wqkv, ("dp", "fsdp"), scatter_dimension=0, tiled=True),
        lax.psum_scatter(grad_bqkv, ("dp", "fsdp"), scatter_dimension=0, tiled=True),
        lax.psum_scatter(grad_wout, ("dp", "fsdp"), scatter_dimension=0, tiled=True),
        lax.psum_scatter(grad_bout, ("dp", "fsdp"), scatter_dimension=0, tiled=True),
        lax.psum_scatter(grad_gain_two, ("dp", "fsdp"), scatter_dimension=0, tiled=True),
        lax.psum_scatter(grad_shift_two, ("dp", "fsdp"), scatter_dimension=0, tiled=True),
        lax.psum_scatter(grad_wup, ("dp", "fsdp"), scatter_dimension=0, tiled=True),
        lax.psum_scatter(grad_bup, ("dp", "fsdp"), scatter_dimension=0, tiled=True),
        lax.psum_scatter(grad_wdown, ("dp", "fsdp"), scatter_dimension=0, tiled=True),
        lax.psum_scatter(grad_bdown, ("dp", "fsdp"), scatter_dimension=0, tiled=True),
    )
    return (
        result,
        grad_inputs,
        shards[0],
        shards[1],
        shards[2],
        shards[3],
        shards[4],
        shards[5],
        shards[6],
        shards[7],
        shards[8],
        shards[9],
        shards[10],
        shards[11],
    )


def solution(mesh):
    in_specs = (
        P(("dp", "fsdp"), None, None),
        P(("dp", "fsdp")),
        P(("dp", "fsdp")),
        P(("dp", "fsdp")),
        P(("dp", "fsdp"), None),
        P(("dp", "fsdp")),
        P(("dp", "fsdp"), None),
        P(("dp", "fsdp")),
        P(("dp", "fsdp")),
        P(("dp", "fsdp")),
        P(("dp", "fsdp"), None),
        P(("dp", "fsdp")),
        P(("dp", "fsdp"), None),
        P(("dp", "fsdp")),
        P(("dp", "fsdp"), None, None),
    )
    out_specs = (
        P(("dp", "fsdp"), None, None),
        P(("dp", "fsdp"), None, None),
        P(("dp", "fsdp")),
        P(("dp", "fsdp")),
        P(("dp", "fsdp"), None),
        P(("dp", "fsdp")),
        P(("dp", "fsdp"), None),
        P(("dp", "fsdp")),
        P(("dp", "fsdp")),
        P(("dp", "fsdp")),
        P(("dp", "fsdp"), None),
        P(("dp", "fsdp")),
        P(("dp", "fsdp"), None),
        P(("dp", "fsdp")),
    )
    return jax.shard_map(body, mesh=mesh, in_specs=in_specs, out_specs=out_specs, check_vma=False)
```

profile of v0, /device:TPU:0, one launch (start us, length us, event | category | flops | bytes accessed | tf_op | source)
XLA Modules:
  0.0 1011.1 jit_solution(6103103956843848803)
XLA Ops:
  16.8 42.7 %all-reduce.17 = (bf16[2304]{0:T(1024)(128)(2,1)S(1)}, bf16[768]{0:T(1024)(128)(2,1)S(1)}, bf16[768]{0:T(1024)(128)(2,1)S(1)}, bf16[768]{0:T(1024)(128)(2,1)S(1)...) all-reduce(bf16[2304]{0:T(1024)(128)(2,1)S(1)} %dynamic-update-slic, ...), channel_id=1, replica_groups=mesh['dp'=4,'fsdp'=8] {'dp','fsdp'}, use_global_device_ids=true, to_apply=%add.2 | all-reduce | flops 9984 | bytes 39936
  64.5 9.5 all-gather.5.cloned.1.call-done
  74.0 7.9 add_convert_fusion
  81.9 6.6 copy.58
  105.8 133.8 %while.28 = (s32[]{:T(128)}, bf16[12,1,1024,64]{2,3,1,0:T(8,128)(2,1)}, f32[12,1,1024]{2,1,0:T(1,128)S(1)}, bf16[12,1,1024,64]{3,2,1,0:T(8,128)(2,1)S(1)}, bf16[...) while((s32[]{:T(128)}, ...), condition=%wide.region_5.6_spmd.clone, body=%wide.region_2.5_spmd.clone.sunk | while | flops 295697408 | bytes 13677657 | solution.py:128
  245.7 10.7 %fusion.117 = f32[1024,3072]{1,0:T(8,128)} fusion(bf16[768,3072]{1,0:T(8,128)(2,1)} %all-gather.9.cloned.1.call-done, f32[1024,768]{0,1:T(8,128)S(1)} %get-tuple-element.296, f32[768]{0:T(1024)S(1)} %convert_element_type.129, f32[768]{0:T(1024)S(1)} %convert_element_type.128, f32[1024]{0:T(1024)S(1)} %add_rsqrt_fusion, f32[1024]{0:T(1024)S(1)} %broadcast_multiply_fusion.4), kind=kOutput, calls=%fused_computation.154 | convolution fusion | flops 4835770368 | bytes 20461568 | tf_op jit(solution)/shard_map/dot_general | solution.py:147
  261.2 17.9 %convert_reduce_fusion = (f32[3072]{0:T(1024)}, bf16[1024,3072]{1,0:T(8,128)(2,1)S(1)}) fusion(f32[1024,3072]{1,0:T(8,128)} %fusion.117, f32[3072]{0:T(1024)S(1)} %convert_element_type.131, bf16[3072,768]{1,0:T(8,128)(2,1)} %all-gather.11.cloned.1.call-done, bf16[1,1024,768]{1,2,0:T(8,128)(2,1)} %copy.63, pred[1024]{0:T(1024)(128)(4,1)S(1)} %get-tuple-element.498), kind=kOutput, calls=%fused_computation.81 | convolution fusion | flops 4906546176 | bytes 25191424 | tf_op jit(solution)/shard_map/rd,fd->rf/dot_general | solution.py:167
  279.1 7.3 fusion.121
  315.0 274.7 %while.29 = (s32[]{:T(128)}, bf16[12,1,1024,64]{2,3,1,0:T(8,128)(2,1)}, bf16[12,1,1024,64]{2,3,1,0:T(8,128)(2,1)}, bf16[12,1,1024,64]{2,3,1,0:T(8,128)(2,1)}, bf...) while((s32[]{:T(128)}, ...), condition=%wide.region_12.13_spmd.clone, body=%wide.region_10.12_spmd.clone.sunk | while | flops 713161728 | bytes 34115696 | solution.py:195
  316.9 5.1 fusion.167
  321.9 5.7 fusion.168
  332.2 5.9 fusion.171
  339.8 5.1 fusion.167
  344.9 5.7 fusion.168
  355.1 5.8 fusion.171
  362.7 5.1 fusion.167
  367.7 5.7 fusion.168
  377.9 5.8 fusion.171
  385.5 5.1 fusion.167
  390.6 5.7 fusion.168
  400.8 5.8 fusion.171
  408.4 5.1 fusion.167
  413.5 5.7 fusion.168
  423.7 5.8 fusion.171
  431.3 5.1 fusion.167
  436.3 5.7 fusion.168
  446.6 5.8 fusion.171
  459.2 5.7 fusion.168
  469.4 5.8 fusion.171
  482.1 5.7 fusion.168
  492.3 5.9 fusion.171
  505.0 5.7 fusion.168
  515.2 5.8 fusion.171
  527.8 5.7 fusion.168
  538.0 5.9 fusion.171
  550.7 5.7 fusion.168
  560.9 5.8 fusion.171
  573.6 5.7 fusion.168
  583.8 5.8 fusion.171
  594.8 6.4 fusion.96
  601.9 10.5 %fusion.116 = f32[768,3072]{1,0:T(8,128)} fusion(bf16[1024,3072]{1,0:T(8,128)(2,1)} %copy-done.27, f32[1024,768]{0,1:T(8,128)S(1)} %get-tuple-element.296, f32[768]{0:T(1024)S(1)} %copy-done.10, f32[768]{0:T(1024)S(1)} %convert_element_type.128, f32[1024]{0:T(1024)S(1)} %add_rsqrt_fusion, f32[1024]{0:T(1024)S(1)} %broadcast_multiply_fusion.4), kind=kOutput, calls=%fused_computation.153 | convolution fusion | flops 4835770368 | bytes 18888704 | tf_op jit(solution)/shard_map/rd,rf->df/dot_general | solution.py:169
  613.0 14.5 %fusion.108 = f32[3072,768]{1,0:T(8,128)} fusion(bf16[1,1024,768]{1,2,0:T(8,128)(2,1)} %copy.63, pred[1024]{0:T(1024)(128)(4,1)S(1)} %get-tuple-element.499, f32[1024,3072]{1,0:T(8,128)} %fusion.117, f32[3072]{0:T(1024)S(1)} %copy-done.21), kind=kOutput, calls=%fused_computation.138 | convolution fusion | flops 4865654784 | bytes 23606272 | tf_op jit(solution)/shard_map/rf,rd->fd/dot_general | solution.py:165
  628.2 9.2 fusion.120
  644.6 42.1 %all-reduce.16 = (f32[768]{0:T(1024)S(1)}, f32[768]{0:T(1024)S(1)}, f32[2304]{0:T(1024)S(1)}, f32[768]{0:T(1024)S(1)}, f32[768]{0:T(1024)S(1)}, /*index=5*/f32[7...) all-reduce(f32[768]{0:T(1024)S(1)} %get-tuple-element.229, ...), channel_id=2, replica_groups=mesh['dp'=4,'fsdp'=8] {'dp','fsdp'}, use_global_device_ids=true, to_apply=%region_16.17.clone | all-reduce | flops 9984 | bytes 79872
  690.3 5.9 fusion.86
  699.8 11.9 %fusion.107 = bf16[1,1024,768]{1,2,0:T(8,128)(2,1)} fusion(f32[1024,768]{0,1:T(8,128)S(1)} %get-tuple-element.296, f32[768]{0:T(1024)S(1)} %convert_element_type.133, bf16[3072,768]{1,0:T(8,128)(2,1)} %all-gather.11.cloned.1.call-done, pred[1024]{0:T(1024)(128)(4,1)S(1)} %get-tuple-element.499, f32[1024,3072]{1,0:T(8,128)} %fusion.117, f32[3072]{0:T(1024)S(1)} %copy-done.21), kind=kOutput, calls=%fused_computation.137 | convolution fusion | flops 4866441216 | bytes 22036480 | tf_op jit(solution)/shard_map/dot_general | solution.py:151
  720.2 141.4 %reduce-scatter.9.cloned.1.call-done = f32[24,3072]{1,0:T(8,128)} async-done(((f32[768,3072]{1,0:T(8,128)}), f32[24,3072]{1,0:T(8,128)}) %reduce-scatter.9.cloned.1.call-update) | async-done | bytes 294928 | tf_op jit(solution)/shard_map/reduce_scatter | solution.py:220
  861.6 142.2 %reduce-scatter.11.cloned.1.call-done = f32[96,768]{1,0:T(8,128)} async-done(((f32[3072,768]{1,0:T(8,128)}), f32[96,768]{1,0:T(8,128)}) %reduce-scatter.11.cloned.1.call-update) | async-done | bytes 294928 | tf_op jit(solution)/shard_map/reduce_scatter | solution.py:222
  (258 shorter events, 339.2 us)
Async XLA Ops:
  7.2 66.8 %all-gather.5.cloned.1.call-start = ((), (), s32[]{:S(2)}) async-start(), calls=%async_computation.4 | async-start | bytes 3649536 | tf_op jit(solution)/shard_map/all_gather | solution.py:106
  7.9 231.7 %all-gather.7.cloned.1.call-start = ((), (), s32[]{:S(2)}) async-start(), calls=%async_computation.5 | async-start | bytes 1216512 | tf_op jit(solution)/shard_map/all_gather | solution.py:108
  8.7 237.0 %all-gather.9.cloned.1.call-start = ((), (), s32[]{:S(2)}) async-start(), calls=%async_computation.6 | async-start | bytes 4866048 | tf_op jit(solution)/shard_map/all_gather | solution.py:135
  9.4 251.8 %all-gather.11.cloned.1.call-start = ((), (), s32[]{:S(2)}) async-start(), calls=%async_computation.7 | async-start | bytes 4866048 | tf_op jit(solution)/shard_map/all_gather | solution.py:137
  10.0 705.4 %reduce-scatter.7.cloned.1.call-start = ((), (), s32[]{:S(2)}) async-start(), calls=%async_computation.9 | async-start | bytes 2433024 | tf_op jit(solution)/shard_map/reduce_scatter | solution.py:216
  59.5 14.5 %copy-start.13 = (f32[768]{0:T(1024)}, f32[768]{0:T(1024)S(1)}, u32[]{:S(2)}) copy-start(f32[768]{0:T(1024)S(1)} %convert_element_type.119) | copy-start | bytes 9220
  59.5 14.5 %copy-start.24 = (f32[768]{0:T(1024)}, f32[768]{0:T(1024)S(1)}, u32[]{:S(2)}) copy-start(f32[768]{0:T(1024)S(1)} %convert_element_type.120) | copy-start | bytes 9220
  59.5 3.4 copy-start.8
  61.4 12.7 %copy-start = (bf16[1,1024,768]{1,2,0:T(8,128)(2,1)}, bf16[1,1024,768]{1,2,0:T(8,128)(2,1)S(1)}, u32[]{:S(2)}) copy-start(bf16[1,1024,768]{1,2,0:T(8,128)(2,1)S(1)} %copy.57) | copy-start | bytes 4718596
  61.7 20.2 %copy-start.11 = (f32[1024]{0:T(1024)}, f32[1024]{0:T(1024)S(1)}, u32[]{:S(2)}) copy-start(f32[1024]{0:T(1024)S(1)} %broadcast_multiply_fusion.5) | copy-start | bytes 12292
  62.1 19.8 %copy-start.15 = (f32[1024]{0:T(1024)}, f32[1024]{0:T(1024)S(1)}, u32[]{:S(2)}) copy-start(f32[1024]{0:T(1024)S(1)} %add_rsqrt_fusion.1) | copy-start | bytes 12292
  62.8 182.9 %copy-start.9 = (f32[768]{0:T(1024)}, f32[768]{0:T(1024)S(1)}, u32[]{:S(2)}) copy-start(f32[768]{0:T(1024)S(1)} %convert_element_type.129) | copy-start | bytes 9220
  62.9 198.3 %copy-start.20 = (f32[3072]{0:T(1024)}, f32[3072]{0:T(1024)S(1)}, u32[]{:S(2)}) copy-start(f32[3072]{0:T(1024)S(1)} %convert_element_type.131) | copy-start | bytes 36868
  239.6 1.6 copy-start.4
  261.2 17.9 %copy-start.6 = (bf16[768,3072]{1,0:T(8,128)(2,1)S(1)}, bf16[768,3072]{1,0:T(8,128)(2,1)}, u32[]{:S(2)}) copy-start(bf16[768,3072]{1,0:T(8,128)(2,1)} %all-gather.9.cloned.1.call-done) | copy-start | bytes 14155780
  279.1 7.3 copy-start.27
  290.0 3.6 copy-start.2
  290.0 3.6 copy-start.5
  295.9 1.7 copy-start.3
  310.9 409.4 %reduce-scatter.5.cloned.1.call-start = ((), (), s32[]{:S(2)}) async-start(), calls=%async_computation.8 | async-start | bytes 7299072 | tf_op jit(solution)/shard_map/reduce_scatter | solution.py:214
  589.7 5.1 copy-start.1
  589.7 5.1 copy-start.12
  589.7 5.1 copy-start.14
  589.7 5.1 copy-start.16
  589.7 5.1 copy-start.25
  592.5 2.2 copy-start.7
  601.2 0.7 copy-start.10
  601.2 260.4 %reduce-scatter.9.cloned.1.call-start = ((), (), s32[]{:S(2)}) async-start(), calls=%async_computation.10 | async-start | bytes 9732096 | tf_op jit(solution)/shard_map/reduce_scatter | solution.py:220
  612.3 0.7 copy-start.21
  612.4 391.4 %reduce-scatter.11.cloned.1.call-start = ((), (), s32[]{:S(2)}) async-start(), calls=%async_computation.11 | async-start | bytes 9732096 | tf_op jit(solution)/shard_map/reduce_scatter | solution.py:222
  627.5 0.7 copy-start.26
  641.1 3.5 copy-start.17
  641.1 3.5 copy-start.18
  641.1 3.6 copy-start.19
  641.1 3.6 copy-start.22
  641.1 3.6 copy-start.23
Sparse Core Ops, SparseCore 0:
  11.0 62.9 all-gather.4
  77.0 53.0 all-gather.6
  133.1 62.6 all-gather.8
  198.7 62.4 all-gather.10
  311.0 97.8 reduce-scatter.6
  601.3 118.8 reduce-scatter.4
  726.7 134.8 reduce-scatter.8
  869.1 134.6 reduce-scatter.10
where the time goes:
time: 1020 us; the launch traced here: 1010 us
  matrix products  403 us (40%)
  waiting for transfers between devices  305 us (30%)
  other arithmetic  133 us (13%)
  blocking collectives  84.8 us (8%)
  local copies, waits for them, and re-layouts  68 us (7%)
  between operations  15.6 us (2%)
    reduce_scatter x1, waiting for transfers between devices, body(): lax.psum_scatter(grad_wdown, ('dp', 'fsdp'), scatter_dimension=0, tiled=T...  142 us
    reduce_scatter x1, waiting for transfers between devices, body(): lax.psum_scatter(grad_wup, ('dp', 'fsdp'), scatter_dimension=0, tiled=True)  141 us
    unnamed x2, blocking collectives  84.8 us
    dot_general x12, matrix products, head_backward(): jnp.einsum('gqk,gqd->gkd', weights.astype(jnp.bfloat16), grad_mixed, pref...  70.2 us
    convert_element_type x12, other arithmetic, head_backward(): grad_low = grad_scores.astype(jnp.bfloat16)  68.2 us
    dot_general x12, matrix products, head_backward(): jnp.einsum('gqd,gkd->gqk', grad_mixed, values, preferred_element_type=jnp...  60.7 us
    dot_general x12, matrix products, head_forward(): jnp.einsum('gqk,gkd->gqd', weighted, values, preferred_element_type=jnp.f...  58 us
    reduce_sum x12, other arithmetic, head_forward(): row_total = jnp.sum(exp_terms, axis=-1, keepdims=True)  45.3 us
  transfers between devices with their start and end apart: 8, of which 5 were waited for; matrix products, arithmetic and copies ran while one was open for 54% of the time, Pallas kernels for 0%

commit v1 on v0

v1 whole, which is shorter than its diff:
```python
import functools
import math

import jax
import jax.numpy as jnp
from jax import lax
from jax.experimental import pallas as pl
from jax.experimental.pallas import tpu as pltpu
from jax.sharding import PartitionSpec as P

H = 12
HD = 64
AXES = ("dp", "fsdp")
NORM_EPS = 1e-05
LOG2E = math.log2(math.e)
NT = (((1,), (1,)), ((), ()))
NN = (((1,), (0,)), ((), ()))
TN = (((0,), (0,)), ((), ()))
bf16 = jnp.bfloat16
f32 = jnp.float32
MIB = 2**20


def dot(a, b, dims):
    return lax.dot_general(a, b, dims, preferred_element_type=f32)


def whole(shape):
    return pl.BlockSpec(shape, lambda *i: (0,) * len(shape), pipeline_mode=pl.Buffered(1))


def smem():
    return pl.BlockSpec(memory_space=pltpu.SMEM)


def params(mib):
    return pltpu.CompilerParams(vmem_limit_bytes=mib * MIB)


def sds(shape, dtype):
    return jax.ShapeDtypeStruct(shape, dtype)


def cost(flops, nbytes):
    return pl.CostEstimate(flops=int(flops), bytes_accessed=int(nbytes), transcendentals=0)


def norm_stats(values):
    mean = jnp.mean(values, axis=1, keepdims=True)
    centred = values - mean
    inverse = lax.rsqrt(jnp.mean(centred * centred, axis=1, keepdims=True) + NORM_EPS)
    return centred * inverse, inverse


def unpack_kernel(pack_ref, *rest, n, rows, layout):
    outs, scratch = rest[:-1], rest[-1]
    scratch[...] = pack_ref[...].astype(f32)
    for d in range(n):
        for out, (row, lane, size) in zip(outs, layout):
            out[:, d * size : (d + 1) * size] = scratch[
                d * rows + row : d * rows + row + 1, lane : lane + size
            ]


def unpack(pack, n, layout):
    total = pack.shape[0]
    return pl.pallas_call(
        functools.partial(unpack_kernel, n=n, rows=total // n, layout=layout),
        out_shape=[sds((1, n * size), f32) for _, _, size in layout],
        scratch_shapes=[pltpu.VMEM(pack.shape, f32)],
        compiler_params=params(16),
    )(pack)


def repack_kernel(*refs, n, layout):
    ins, out = refs[:-1], refs[-1]
    out[...] = jnp.zeros_like(out)
    for d in range(n):
        for ref, (row, lane, size) in zip(ins, layout):
            out[d, row : row + 1, lane : lane + size] = ref[:, d * size : (d + 1) * size]


def repack(vectors, n, layout):
    return pl.pallas_call(
        functools.partial(repack_kernel, n=n, layout=layout),
        out_shape=sds((n, 8, 128), f32),
        compiler_params=params(16),
    )(*vectors)


def qkv_kernel(x_ref, g_ref, b_ref, w_ref, bq_ref, a_ref, o_ref):
    normal, _ = norm_stats(x_ref[...].astype(f32))
    a = (normal * g_ref[...] + b_ref[...]).astype(bf16)
    a_ref[...] = a
    o_ref[...] = (dot(a, w_ref[...], NN) + bq_ref[...]).astype(bf16)


def qkv_call(x, gain, bias, w, bq, rb=256):
    s, d = x.shape
    e = bq.shape[1]
    return pl.pallas_call(
        qkv_kernel,
        grid=(s // rb,),
        in_specs=[
            pl.BlockSpec((rb, d), lambda i: (i, 0)),
            whole((1, d)),
            whole((1, d)),
            whole((d, e)),
            whole((1, e)),
        ],
        out_specs=[pl.BlockSpec((rb, d), lambda i: (i, 0)), pl.BlockSpec((rb, e), lambda i: (i, 0))],
        out_shape=[sds((s, d), bf16), sds((s, e), bf16)],
        compiler_params=params(40),
        cost_estimate=cost(2 * s * d * e, 2 * d * e + 2 * s * (2 * d + e)),
    )(x, gain, bias, w, bq)


def fwd_kernel(len_ref, q_ref, k_ref, v_ref, o_ref, rz_ref, *kept, qb, nq):
    p_refs, a_refs = kept[:nq], kept[nq:]
    n = len_ref[0]
    c = HD ** (-0.5) * LOG2E
    lane = lax.broadcasted_iota(jnp.int32, (1, 128), 1)
    for i in range(nq):
        rows = slice(i * qb, (i + 1) * qb)

        @pl.when(n > i * qb)
        def _():
            nk = (i + 1) * qb
            q = q_ref[rows, :]
            k = k_ref[:nk, :]
            v = v_ref[:nk, :]
            row = lax.broadcasted_iota(jnp.int32, (qb, qb), 0)
            col = lax.broadcasted_iota(jnp.int32, (qb, qb), 1)
            mask = (col <= row) & (col < n - i * qb)
            mixed = []
            inverse_total = []
            for h in range(2):
                mine = (lane < HD) if h == 0 else (lane >= HD)
                scores = dot(jnp.where(mine, q, jnp.zeros_like(q)), k, NT) * c
                square = scores * scores + LOG2E * LOG2E
                top = jnp.max(jnp.where(mask, square[:, i * qb :], 0.0), axis=1, keepdims=True)
                if i:
                    top = jnp.maximum(top, jnp.max(square[:, : i * qb], axis=1, keepdims=True))
                inv = lax.rsqrt(square)
                e = jnp.exp2(square * inv - jnp.sqrt(top))
                last = jnp.where(mask, e[:, i * qb :], 0.0)
                e = jnp.concatenate([e[:, : i * qb], last], axis=1) if i else last
                total = jnp.sum(e, axis=1, keepdims=True)
                p = (scores * inv * e).astype(bf16)
                inv = inv * LOG2E
                p_refs[i][h] = p
                a_refs[i][h] = ((1.0 - inv * inv * (1.0 - inv)) * e).astype(bf16)
                rz = 1.0 / total
                mixed.append(dot(p, v, NN) * rz)
                inverse_total.append(rz)
            o_ref[rows, :] = jnp.where(lane < HD, mixed[0], mixed[1]).astype(bf16)
            rz_ref[rows, :] = jnp.where(lane < HD, inverse_total[0], inverse_total[1])

        @pl.when(n <= i * qb)
        def _():
            o_ref[rows, :] = jnp.zeros((qb, 128), bf16)
            rz_ref[rows, :] = jnp.zeros((qb, 128), f32)


def attention_forward(lens, qkv, qb=256, first=0, groups=H // 2):
    s = qkv.shape[0]
    nq = s // qb
    hp = H // 2

    def columns(off):
        return pl.BlockSpec((s, 128), lambda g: (0, first + g + off))

    kept_shape = [sds((2 * groups, qb, (i + 1) * qb), bf16) for i in range(nq)]
    kept_spec = [pl.BlockSpec((2, qb, (i + 1) * qb), lambda g: (g, 0, 0)) for i in range(nq)]
    return pl.pallas_call(
        functools.partial(fwd_kernel, qb=qb, nq=nq),
        grid=(groups,),
        in_specs=[smem(), columns(0), columns(hp), columns(2 * hp)],
        out_specs=[pl.BlockSpec((s, 128), lambda g: (0, g))] * 2 + kept_spec * 2,
        out_shape=[sds((s, 128 * groups), bf16), sds((s, 128 * groups), f32)] + kept_shape * 2,
        compiler_params=params(48),
        cost_estimate=cost(groups * 6e9, groups * 6e6),
    )(lens, qkv, qkv, qkv)


def bwd_kernel(len_ref, q_ref, k_ref, v_ref, o_ref, rz_ref, d_ref, *rest, qb, nq):
    p_refs, a_refs = rest[:nq], rest[nq : 2 * nq]
    out, dk_ref, dv_ref = rest[2 * nq :]
    n = len_ref[0]
    scale = HD ** (-0.5)
    lane = lax.broadcasted_iota(jnp.int32, (1, 128), 1)
    dk_ref[...] = jnp.zeros_like(dk_ref)
    dv_ref[...] = jnp.zeros_like(dv_ref)
    for i in range(nq):
        rows = slice(i * qb, (i + 1) * qb)

        @pl.when(n > i * qb)
        def _():
            nk = (i + 1) * qb
            q = q_ref[rows, :]
            k = k_ref[:nk, :]
            v = v_ref[:nk, :]
            grad = d_ref[rows, :] * rz_ref[rows, :]
            low = grad.astype(bf16)
            along = grad * o_ref[rows, :].astype(f32)
            low_t = low.T
            q_t = q.T
            dq = []
            for h in range(2):
                mine = (lane < HD) if h == 0 else (lane >= HD)
                part = slice(h * HD, (h + 1) * HD)
                total = jnp.sum(jnp.where(mine, along, 0.0), axis=1, keepdims=True)
                dp = dot(jnp.where(mine, low, jnp.zeros_like(low)), v, NT)
                p = p_refs[i][h]
                ds = (a_refs[i][h].astype(f32) * dp - p.astype(f32) * total).astype(bf16)
                dq.append(dot(ds, k, NN))
                dv_ref[part, :nk] += dot(low_t[part, :], p, NN)
                dk_ref[part, :nk] += dot(q_t[part, :], ds, NN)
            out[0, rows, :] = (jnp.where(lane < HD, dq[0], dq[1]) * scale).astype(bf16)

        @pl.when(n <= i * qb)
        def _():
            out[0, rows, :] = jnp.zeros((qb, 128), bf16)

    out[1] = (dk_ref[...] * scale).T.astype(bf16)
    out[2] = dv_ref[...].T.astype(bf16)


def attention_backward(lens, qkv, o, rz, dol, kept, qb=256, first=0, groups=H // 2):
    s = qkv.shape[0]
    nq = s // qb
    hp = H // 2

    def columns(off):
        return pl.BlockSpec((s, 128), lambda g: (0, first + g + off))

    kept_spec = [pl.BlockSpec((2, qb, (i + 1) * qb), lambda g: (first + g, 0, 0)) for i in range(nq)]
    return pl.pallas_call(
        functools.partial(bwd_kernel, qb=qb, nq=nq),
        grid=(groups,),
        in_specs=[smem(), columns(0), columns(hp), columns(2 * hp)] + [columns(0)] * 3 + kept_spec * 2,
        out_specs=pl.BlockSpec((3, s, 128), lambda g: (0, 0, g)),
        out_shape=sds((3, s, 128 * groups), bf16),
        scratch_shapes=[pltpu.VMEM((128, s), f32)] * 2,
        compiler_params=params(48),
        cost_estimate=cost(groups * 4e9, groups * 6e6),
    )(lens, qkv, qkv, qkv, o, rz, dol, *kept)


def ffn_kernel(
    len_ref, x_ref, o_ref, ct_ref, wo_ref, *rest, rb, n, nu
):
    wu_refs, wd_refs = rest[:nu], rest[nu : 2 * nu]
    bo_ref, g2_ref, b2_ref, bu_ref, bd_ref = rest[2 * nu : 2 * nu + 5]
    (y_ref, g_ref, du_ref, c_ref, dyl_ref, drl_ref, dr_ref, dol_ref) = rest[2 * nu + 5 : 2 * nu + 13]
    sbd, sbu, sg2, sb2, sbo, wd = rest[2 * nu + 13 :]
    i = pl.program_id(0)
    d = x_ref.shape[1]
    each = d // n

    @pl.when(i == 0)
    def _():
        for s in (sbd, sbu, sg2, sb2, sbo):
            s[...] = jnp.zeros_like(s)
        for dev in range(n):
            for j in range(nu):
                at = (dev * nu + j) * each
                wd[at : at + each, :] = wd_refs[j][dev * each : (dev + 1) * each, :]

    live = (lax.broadcasted_iota(jnp.int32, (rb, 1), 0) + i * rb) < len_ref[0]
    r = x_ref[...].astype(f32) + dot(o_ref[...], wo_ref[...], NN) + bo_ref[...]
    n2, k2 = norm_stats(r)
    g2 = g2_ref[...]
    c = (n2 * g2 + b2_ref[...]).astype(bf16)
    c_ref[...] = c
    dyl = jnp.where(live, ct_ref[...], jnp.zeros((), bf16))
    dyl_ref[...] = dyl
    y = r + bd_ref[...]
    dc = jnp.zeros_like(r)
    k0 = math.sqrt(2 / math.pi)
    for j in range(nu):
        cols = slice(j * d, (j + 1) * d)
        wu = wu_refs[j][...]
        wdj = wd[cols, :]
        u = dot(c, wu, NN) + bu_ref[:, cols]
        t = dot(dyl, wdj, NT)
        u2 = u * u
        hp = 0.5 + 0.5 * jnp.tanh(u * (k0 + (k0 * 0.044715) * u2))
        g = (u * hp).astype(bf16)
        slope = hp + u * (2.0 * hp * (1.0 - hp)) * (k0 + (3 * k0 * 0.044715) * u2)
        du = (t * slope).astype(bf16)
        g_ref[:, cols] = g
        du_ref[:, cols] = du
        y = y + dot(g, wdj, NN)
        dc = dc + dot(du, wu, NT)
        sbu[:, cols] += jnp.sum(du.astype(f32), axis=0, keepdims=True)
    y_ref[...] = jnp.where(live, y, 0.0).astype(bf16)
    q2 = dc * g2
    inner = q2 - jnp.mean(q2, axis=1, keepdims=True) - n2 * jnp.mean(q2 * n2, axis=1, keepdims=True)
    dr = dyl.astype(f32) + k2 * inner
    dr_ref[...] = dr
    drl = dr.astype(bf16)
    drl_ref[...] = drl
    dol_ref[...] = dot(drl, wo_ref[...], NT)
    sbd[...] += jnp.sum(dyl.astype(f32), axis=0, keepdims=True)
    sg2[...] += jnp.sum(dc * n2, axis=0, keepdims=True)
    sb2[...] += jnp.sum(dc, axis=0, keepdims=True)
    sbo[...] += jnp.sum(drl.astype(f32), axis=0, keepdims=True)


def ffn_call(lens, x, o, ct, weights, bo, g2, b2, bu, bd, n, first, rb=256):
    s, d = x.shape
    ff = bu.shape[1]
    nu = ff // d

    def row(w):
        return pl.BlockSpec((rb, w), lambda i: (i, 0))

    def acc(w):
        return pl.BlockSpec((1, w), lambda i: (0, 0))

    def part(j):
        return pl.BlockSpec((d, d), lambda i: (0, first + j), pipeline_mode=pl.Buffered(1))

    return pl.pallas_call(
        functools.partial(ffn_kernel, rb=rb, n=n, nu=nu),
        grid=(s // rb,),
        in_specs=[smem(), row(d), row(d), row(d)]
        + [part(j) for j in range(1 + 2 * nu)]
        + [whole((1, d)), whole((1, d)), whole((1, d)), whole((1, ff)), whole((1, d))],
        out_specs=[row(d), row(ff), row(ff), row(d), row(d), row(d), row(d), row(d)]
        + [acc(d), acc(ff), acc(d), acc(d), acc(d)],
        out_shape=[
            sds((s, d), bf16),
            sds((s, ff), bf16),
            sds((s, ff), bf16),
            sds((s, d), bf16),
            sds((s, d), bf16),
            sds((s, d), bf16),
            sds((s, d), f32),
            sds((s, d), f32),
            sds((1, d), f32),
            sds((1, ff), f32),
            sds((1, d), f32),
            sds((1, d), f32),
            sds((1, d), f32),
        ],
        scratch_shapes=[pltpu.VMEM((ff, d), bf16)],
        compiler_params=params(56),
        cost_estimate=cost(8 * s * d * ff + 4 * s * d * d, 4 * d * ff + 4 * s * ff + 20 * s * d),
    )(lens, x, o, ct, *([weights] * (1 + 2 * nu)), bo, g2, b2, bu, bd)


def wgrad_kernel(a_ref, b_ref, o_ref):
    b = b_ref[0] if len(b_ref.shape) == 3 else b_ref[...]
    o_ref[...] = dot(a_ref[...], b, TN).astype(o_ref.dtype)


def wgrad(a, b, ta, tb):
    s, m = a.shape
    if b.ndim == 3:
        n = b.shape[0] * b.shape[2]
        b_spec = pl.BlockSpec((1, s, b.shape[2]), lambda i, j: (j, 0, 0))
        tb = b.shape[2]
    else:
        n = b.shape[1]
        b_spec = pl.BlockSpec((s, tb), lambda i, j: (0, j))
    return pl.pallas_call(
        wgrad_kernel,
        grid=(m // ta, n // tb),
        in_specs=[pl.BlockSpec((s, ta), lambda i, j: (0, i)), b_spec],
        out_specs=pl.BlockSpec((ta, tb), lambda i, j: (i, j)),
        out_shape=sds((m, n), bf16),
        compiler_params=params(40),
        cost_estimate=cost(2 * s * m * n, 2 * (s * m + s * n + m * n)),
    )(a, b)


def first_kernel(x_ref, dr_ref, dq_ref, w_ref, g_ref, gi_ref, sg, sb, sq):
    i = pl.program_id(0)

    @pl.when(i == 0)
    def _():
        for s in (sg, sb, sq):
            s[...] = jnp.zeros_like(s)

    normal, inverse = norm_stats(x_ref[...].astype(f32))
    d = x_ref.shape[1]
    da = jnp.zeros(normal.shape, f32)
    for j in range(3):
        part = dq_ref[j]
        da = da + dot(part, w_ref[:, j * d : (j + 1) * d], NT)
        sq[:, j * d : (j + 1) * d] += jnp.sum(part.astype(f32), axis=0, keepdims=True)
    q1 = da * g_ref[...]
    inner = (
        q1 - jnp.mean(q1, axis=1, keepdims=True) - normal * jnp.mean(q1 * normal, axis=1, keepdims=True)
    )
    gi_ref[...] = dr_ref[...] + inverse * inner
    sg[...] += jnp.sum(da * normal, axis=0, keepdims=True)
    sb[...] += jnp.sum(da, axis=0, keepdims=True)


def first_backward(x, dr, dqkv, w, gain, rb=256):
    s, d = x.shape
    e = 3 * d

    def row(w):
        return pl.BlockSpec((rb, w), lambda i: (i, 0))

    def acc(w):
        return pl.BlockSpec((1, w), lambda i: (0, 0))

    return pl.pallas_call(
        first_kernel,
        grid=(s // rb,),
        in_specs=[row(d), row(d), pl.BlockSpec((3, rb, d), lambda i: (0, i, 0)), whole((d, e)), whole((1, d))],
        out_specs=[row(d), acc(d), acc(d), acc(e)],
        out_shape=[sds((s, d), f32), sds((1, d), f32), sds((1, d), f32), sds((1, e), f32)],
        compiler_params=params(40),
        cost_estimate=cost(2 * s * d * e, 2 * d * e + 16 * s * d),
    )(x, dr, dqkv, w, gain)


def scatter_sum(buf, n, order):
    lin = lax.axis_index(AXES)
    bits = n.bit_length() - 1
    rest = buf.shape[1:]
    buf = buf.reshape((2,) * bits + rest)
    left = list(range(bits - 1, -1, -1))
    for step, b in enumerate(order):
        axis = left.index(b)
        left.pop(axis)
        bit = (lin >> b) & 1
        send = lax.dynamic_index_in_dim(buf, 1 - bit, axis, keepdims=False)
        keep = lax.dynamic_index_in_dim(buf, bit, axis, keepdims=False)
        got = lax.ppermute(send, AXES, [(i, i ^ (1 << b)) for i in range(n)])
        buf = keep.astype(f32) + got.astype(f32)
        if step < bits - 1:
            buf = buf.astype(send.dtype)
    return buf


def body(
    n,
    dp,
    layer_input,
    lengths,
    ln1_gain,
    ln1_bias,
    w_qkv,
    b_qkv,
    w_out,
    b_out,
    ln2_gain,
    ln2_bias,
    w_up,
    b_up,
    w_down,
    b_down,
    cotangent,
):
    s, d = layer_input.shape[1:]
    x = layer_input.reshape(s, d)
    ct = cotangent.reshape(s, d)
    e, ff = w_qkv.shape[1], w_up.shape[1]
    each = d // n
    nu = ff // d
    vectors = (ln1_gain, ln1_bias, b_out, ln2_gain, ln2_bias, b_down, b_qkv, b_up)
    if each >= 4:
        layout = [(2, each * k, each) for k in range(5)] + [(3, 0, each), (0, 0, 3 * each), (1, 0, nu * each)]
    else:
        layout = [(0, each * k, each) for k in range(6)] + [(1, 0, 3 * each), (1, 64, nu * each)]
    rows = [
        [(lane, size, vec) for (row, lane, size), vec in zip(layout, vectors) if row == r] for r in range(each)
    ]
    packed = []
    for row in rows:
        pieces, at = [], 0
        for lane, size, vec in sorted(row, key=lambda t: t[0]):
            if lane > at:
                pieces.append(jnp.zeros((lane - at,), bf16))
            pieces.append(vec)
            at = lane + size
        pieces.append(jnp.zeros((128 - at,), bf16))
        packed.append(jnp.concatenate(pieces))
    pack = jnp.stack(packed)
    down = [w_down[j * each : (j + 1) * each] for j in range(nu)]
    block = jnp.concatenate([w_qkv, w_out, w_up, *down, pack], axis=1)
    gathered = lax.all_gather(block, AXES, axis=0, tiled=True)
    wide = e + d + 2 * ff
    g1, b1, bo, g2, b2, bd, bq, bu = unpack(gathered[:, wide:], n, layout)

    a, qkv = qkv_call(x, g1, b1, gathered, bq)
    o, rz, *kept = attention_forward(lengths, qkv)
    (y, g, du, c, dyl, drl, dr, dol, sbd, sbu, sg2, sb2, sbo) = ffn_call(
        lengths, x, o, ct, gathered, bo, g2, b2, bu, bd, n, e // d
    )
    order = list(range(n.bit_length() - 1))
    fs = (n // dp).bit_length() - 1
    order = [0] + order[fs:] + order[1:fs]
    dw_down = wgrad(g, dyl, 768, d)
    grad_down = scatter_sum(dw_down.reshape(n, ff // n, d), n, order)
    dw_up = wgrad(c, du, d, 768)
    grad_up = scatter_sum(dw_up.reshape(n, each, ff), n, order)
    dw_out = wgrad(o, drl, d, d)
    grad_out = scatter_sum(dw_out.reshape(n, each, d), n, order)
    dqkv = attention_backward(lengths, qkv, o, rz, dol, kept)
    dw_qkv = wgrad(a, dqkv, d, d)
    grad_qkv = scatter_sum(dw_qkv.reshape(n, each, e), n, order)
    grad_input, sg1, sb1, sbq = first_backward(x, dr, dqkv, gathered, g1)
    small = repack((sg1, sb1, sbo, sg2, sb2, sbd, sbq, sbu), n, layout)
    small = scatter_sum(small, n, order)
    gs1, gb1, gbo, gs2, gb2, gbd, gbq, gbu = [small[r, lane : lane + size] for r, lane, size in layout]
    return (
        y.reshape(layer_input.shape),
        grad_input.reshape(layer_input.shape),
        gs1,
        gb1,
        grad_qkv,
        gbq,
        grad_out,
        gbo,
        gs2,
        gb2,
        grad_up,
        gbu,
        grad_down,
        gbd,
    )


def solution(mesh):
    split = P(AXES)
    wide = P(AXES, None)
    cube = P(AXES, None, None)
    in_specs = (
        cube, split, split, split, wide, split, wide, split, split, split, wide, split, wide, split, cube,
    )
    out_specs = (
        cube, cube, split, split, wide, split, wide, split, split, split, wide, split, wide, split,
    )
    n = mesh.shape["dp"] * mesh.shape["fsdp"]
    return jax.shard_map(
        functools.partial(body, n, mesh.shape["dp"]),
        mesh=mesh,
        in_specs=in_specs,
        out_specs=out_specs,
        check_vma=False,
    )
```

time: 1020 us -> 407 us (0.40)
  matrix products: 403 us -> 0 us
  other arithmetic: 133 us -> 8.23 us
  Pallas kernels: 0 us -> 120 us
  waiting for transfers between devices: 305 us -> 189 us
  blocking collectives: 84.8 us -> 0 us
  starting transfers between devices: 0.53 us -> 42.7 us
  local copies, waits for them, and re-layouts: 68 us -> 31.7 us
    dot_general x96 -> x0, matrix products: 403 us -> none  [the longest x12 70.2 us: head_backward(): jnp.einsum('gqk,gqd->gkd', weights.astype(jnp.bfloat16), grad_mixed, pref...]
    reduce_scatter x4 -> x0, waiting for transfers between devices: 288 us -> none  [the longest x1 142 us: body(): lax.psum_scatter(grad_wdown, ('dp', 'fsdp'), scatter_dimension=0, tiled=T...]
    pallas_call x0 -> x11, Pallas kernels: none -> 120 us  [the longest x1 36.5 us: ffn_call(): pl.pallas_call(functools.partial(ffn_kernel, rb=rb, n=n, nu=nu), grid=(s...]
    all_gather x4 -> x1, waiting for transfers between devices: 14.3 us -> 106 us  [body(): gathered = lax.all_gather(block, AXES, axis=0, tiled=True)]
    unnamed x2 -> x0, blocking collectives: 84.8 us -> none
    ppermute x0 -> x25, waiting for transfers between devices: none -> 83 us  [scatter_sum(): got = lax.ppermute(send, AXES, [(i, i ^ 1 << b) for i in range(n)])]
    convert_element_type x20 -> x16, other arithmetic: 68.2 us -> 5.35 us  [scatter_sum(): buf = buf.astype(send.dtype)]
    reduce_sum x19 -> x0, other arithmetic: 58.6 us -> none  [the longest x12 45.3 us: head_forward(): row_total = jnp.sum(exp_terms, axis=-1, keepdims=True)]
  transfers between devices with their start and end apart: 8 -> 26, of which waited for: 5 -> 16; matrix products, arithmetic and copies ran while one was open for 54% -> 3% of each run, Pallas kernels for 0% -> 5%
where the time goes in v1:
time: 407 us
  waiting for transfers between devices  189 us (46%)
  Pallas kernels  120 us (29%)
  starting transfers between devices  42.7 us (10%)
  local copies, waits for them, and re-layouts  31.7 us (8%)
  between operations  15.3 us (4%)
  other arithmetic  8.23 us (2%)
    all_gather x1, waiting for transfers between devices, body(): gathered = lax.all_gather(block, AXES, axis=0, tiled=True)  106 us
    ppermute x25, waiting for transfers between devices, scatter_sum(): got = lax.ppermute(send, AXES, [(i, i ^ 1 << b) for i in range(n)])  83 us
    ppermute x25, starting transfers between devices, scatter_sum(): got = lax.ppermute(send, AXES, [(i, i ^ 1 << b) for i in range(n)])  42.6 us
    pallas_call x1, Pallas kernels, ffn_call(): pl.pallas_call(functools.partial(ffn_kernel, rb=rb, n=n, nu=nu), grid=(s...  36.5 us
    pallas_call x1, Pallas kernels, attention_forward(): pl.pallas_call(functools.partial(fwd_kernel, qb=qb, nq=nq), grid=(groups,...  26.8 us
    unnamed x65, local copies, waits for them, and re-layouts  20.9 us
    pallas_call x1, Pallas kernels, attention_backward(): pl.pallas_call(functools.partial(bwd_kernel, qb=qb, nq=nq), grid=(groups,...  20.8 us
    pallas_call x4, Pallas kernels, wgrad(): pl.pallas_call(wgrad_kernel, grid=(m // ta, n // tb), in_specs=[pl.BlockS...  19.1 us
  transfers between devices with their start and end apart: 26, of which 16 were waited for; matrix products, arithmetic and copies ran while one was open for 3% of the time, Pallas kernels for 5%

profile of v1, /device:TPU:0, one launch (start us, length us, event | category | flops | bytes accessed | tf_op | source)
XLA Modules:
  0.0 407.2 jit_solution(5590136972121293286)
XLA Ops:
  7.2 1.0 constant_dynamic-update-slice_fusion.3
  14.4 3.4 concatenate.17
  19.3 106.3 %all-gather.2.cloned.1.call-done.w_ref.wo_ref.rest_0_.rest_1_.rest_2_.rest_3_.rest_4_.rest_5_.rest_6_.rest_7_ = bf16[768,9344]{1,0:T(8,128)(2,1)} async-done(((bf16[24,9344]{1,0:T(8,128)(2,1)}), bf16[768,9344]{1,0:T(8,128)(2,1)}) %all-gather.2.cloned.1.call-update) | async-done | bytes 14352400 | tf_op jit(solution)/shard_map/all_gather | solution.py:489
  125.6 0.9 slice.52.pack_ref
  129.7 7.2 %shard_map.255 = (bf16[1024,768]{1,0:T(8,128)(2,1)S(1)}, bf16[1024,2304]{1,0:T(8,128)(2,1)S(1)}) custom-call(bf16[1024,768]{1,0:T(8,128)(2,1)S(1)} %bitcast.170, f32[1,768]{1,0:T(1,128)S(1)} %get-tuple-element.51.g_ref, f32[1,768]{1,0:T(1,128)S(1)} %get-tuple-element.52.b_ref, ...), custom_call_target="tpu_custom_call" | custom-call | flops 3623878656 | bytes 11403264 | tf_op jit(solution)/shard_map/pallas_call | solution.py:101
  137.0 2.1 copy-done.18
  139.1 1.2 copy-done.21
  140.3 26.8 %shard_map.256 = (bf16[1024,768]{1,0:T(8,128)(2,1)S(1)}, f32[1024,768]{1,0:T(8,128)}, bf16[12,256,256]{2,1,0:T(8,128)(2,1)S(1)}, bf16[12,256,512]{2,1,0:T(8,128)...) custom-call(s32[1]{0:T(128)S(6)} %copy.81.len_ref, ...), custom_call_target="tpu_custom_call" | custom-call | flops 35999997952 | bytes 36000000 | tf_op jit(solution)/shard_map/pallas_call | solution.py:175
  167.0 1.1 copy-done.5
  168.1 36.5 %shard_map.257 = (bf16[1024,768]{1,0:T(8,128)(2,1)}, bf16[1024,3072]{1,0:T(8,128)(2,1)}, bf16[1024,3072]{1,0:T(8,128)(2,1)}, bf16[1024,768]{1,0:T(8,128)(2,1)}, ...) custom-call(s32[1]{0:T(128)S(6)} %copy.81.len_ref, ...), custom_call_target="tpu_custom_call" | custom-call | flops 21743271936 | bytes 37748736 | tf_op jit(solution)/shard_map/pallas_call | solution.py:325
  204.7 1.4 copy-done.25
  206.1 20.8 %shard_map.258.dq_ref.b_ref = bf16[3,1024,768]{2,1,0:T(8,128)(2,1)} custom-call(s32[1]{0:T(128)S(6)} %copy.81.len_ref, bf16[1024,2304]{1,0:T(8,128)(2,1)} %copy-done.18, bf16[1024,2304]{1,0:T(8,128)(2,1)} %copy-done.18, bf16[1024,2304]{1,0:T(8,128)(2,1)} %copy-done.18, bf16[1024,768]{1,0:T(8,128)(2,1)S(1)} %copy-done.6, ...), custom_call_target="tpu_custom_call" | custom-call | flops 24000000000 | bytes 36000000 | tf_op jit(solution)/shard_map/pallas_call | solution.py:238
  226.9 2.3 copy-done.2
  229.3 8.9 %shard_map.259 = (f32[1024,768]{1,0:T(8,128)}, f32[1,768]{1,0:T(1,128)S(1)}, f32[1,768]{1,0:T(1,128)S(1)}, f32[1,2304]{1,0:T(1,128)S(1)}) custom-call(bf16[1024,768]{1,0:T(8,128)(2,1)S(1)} %bitcast.171, f32[1024,768]{1,0:T(8,128)S(1)} %copy-done.4, bf16[3,1024,768]{2,1,0:T(8,128)(2,1)S(1)} %copy-done.2, ...), custom_call_target="tpu_custom_call" | custom-call | flops 3623878656 | bytes 16121856 | tf_op jit(solution)/shard_map/pallas_call | solution.py:413
  238.8 4.7 %shard_map.261 = bf16[768,2304]{1,0:T(8,128)(2,1)S(1)} custom-call(bf16[1024,768]{1,0:T(8,128)(2,1)S(1)} %copy-done.22, bf16[3,1024,768]{2,1,0:T(8,128)(2,1)S(1)} %copy-done.3), custom_call_target="tpu_custom_call" | custom-call | flops 3623878656 | bytes 9830400 | tf_op jit(solution)/shard_map/pallas_call | solution.py:368
  243.8 1.4 copy.71
  245.8 1.4 shard_map.262
  247.8 1.5 collective-permute-start.1
  249.3 2.8 copy-done.17
  252.1 6.5 %shard_map.263 = bf16[768,3072]{1,0:T(8,128)(2,1)S(1)} custom-call(bf16[1024,768]{1,0:T(8,128)(2,1)S(1)} %copy-done.20, bf16[1024,3072]{1,0:T(8,128)(2,1)S(1)} %copy-done.17), custom_call_target="tpu_custom_call" | custom-call | flops 4831838208 | bytes 12582912 | tf_op jit(solution)/shard_map/pallas_call | solution.py:368
  258.6 19.0 %collective-permute-start.2 = (f32[2,2,8,128]{3,2,1,0:T(8,128)S(1)}, f32[2,2,8,128]{3,2,1,0:T(8,128)S(1)}, u32[]{:S(2)}, u32[]{:S(2)}) collective-permute-start(f32[2,2,8,128]{3,2,1,0:T(8,128)S(1)} %dynamic-slice_bitcast_fusion.17), channel_id=1, source_target_pairs={{0,16},{1,17},{2,18},{3,19},{4,20},{5,21},{6,22},{7,23},{8,24},{9,... | collective-permute-start | bytes 49160 | tf_op jit(solution)/shard_map/ppermute | solution.py:436
  278.2 1.1 collective-permute-done.2
  279.3 2.0 collective-permute-start.3
  281.4 6.5 %shard_map.264 = bf16[3072,768]{1,0:T(8,128)(2,1)S(1)} custom-call(bf16[1024,3072]{1,0:T(8,128)(2,1)S(1)} %bitcast.178, bf16[1024,768]{1,0:T(8,128)(2,1)S(1)} %copy-done.19), custom_call_target="tpu_custom_call" | custom-call | flops 4831838208 | bytes 12582912 | tf_op jit(solution)/shard_map/pallas_call | solution.py:368
  288.4 1.8 collective-permute-start.11
  290.7 1.7 collective-permute-done.4
  292.5 3.6 collective-permute-done.11
  296.1 1.3 collective-permute-start.12
  298.0 3.3 collective-permute-done.12
  301.4 1.3 collective-permute-start.13
  302.7 1.9 fusion.2
  304.7 1.7 collective-permute-start.6
  307.0 1.4 collective-permute-start.14
  308.9 3.4 collective-permute-done.14
  312.9 9.9 %collective-permute-done.6 = bf16[2,2,2,24,2304]{4,3,1,2,0:T(8,128)(2,1)S(1)} collective-permute-done((bf16[2,2,2,24,2304]{4,3,1,2,0:T(8,128)(2,1)S(1)}, bf16[2,2,2,24,2304]{4,3,1,2,0:T(8,128)(2,1)S(1)}, u32[]{:S(2)}, u32[]{:S(2)}) %collective-permute-start.6) | collective-permute-done | bytes 884768 | tf_op jit(solution)/shard_map/ppermute | solution.py:436
  323.1 1.4 collective-permute-start.7
  325.6 1.2 collective-permute-start.16
  326.7 4.7 %collective-permute-done.7 = bf16[2,2,24,2304]{3,2,0,1:T(8,128)(2,1)S(1)} collective-permute-done((bf16[2,2,24,2304]{3,2,0,1:T(8,128)(2,1)S(1)}, bf16[2,2,24,2304]{3,2,0,1:T(8,128)(2,1)S(1)}, u32[]{:S(2)}, u32[]{:S(2)}) %collective-permute-start.7) | collective-permute-done | bytes 442400 | tf_op jit(solution)/shard_map/ppermute | solution.py:436
  333.1 1.5 collective-permute-start.21
  334.6 4.2 %collective-permute-done.8 = bf16[2,24,2304]{2,1,0:T(8,128)(2,1)S(1)} collective-permute-done((bf16[2,24,2304]{2,1,0:T(8,128)(2,1)S(1)}, bf16[2,24,2304]{2,1,0:T(8,128)(2,1)S(1)}, u32[]{:S(2)}, u32[]{:S(2)}) %collective-permute-start.8) | collective-permute-done | bytes 221216 | tf_op jit(solution)/shard_map/ppermute | solution.py:436
  339.7 14.8 %collective-permute-done.16 = bf16[2,2,2,24,3072]{4,3,1,2,0:T(8,128)(2,1)S(1)} collective-permute-done((bf16[2,2,2,24,3072]{4,3,1,2,0:T(8,128)(2,1)S(1)}, bf16[2,2,2,24,3072]{4,3,1,2,0:T(8,128)(2,1)S(1)}, u32[]{:S(2)}, u32[]{:S(2)}) %collective-permute-start.16) | collective-permute-done | bytes 1179680 | tf_op jit(solution)/shard_map/ppermute | solution.py:436
  356.4 17.4 %collective-permute-done.21 = bf16[2,2,2,96,768]{4,3,1,2,0:T(8,128)(2,1)S(1)} collective-permute-done((bf16[2,2,2,96,768]{4,3,1,2,0:T(8,128)(2,1)S(1)}, bf16[2,2,2,96,768]{4,3,1,2,0:T(8,128)(2,1)S(1)}, u32[]{:S(2)}, u32[]{:S(2)}) %collective-permute-start.21) | collective-permute-done | bytes 1179680 | tf_op jit(solution)/shard_map/ppermute | solution.py:436
  374.2 1.0 collective-permute-start.22
  376.0 8.1 %collective-permute-done.22 = bf16[2,2,96,768]{3,2,0,1:T(8,128)(2,1)S(1)} collective-permute-done((bf16[2,2,96,768]{3,2,0,1:T(8,128)(2,1)S(1)}, bf16[2,2,96,768]{3,2,0,1:T(8,128)(2,1)S(1)}, u32[]{:S(2)}, u32[]{:S(2)}) %collective-permute-start.22) | collective-permute-done | bytes 589856 | tf_op jit(solution)/shard_map/ppermute | solution.py:436
  386.6 5.1 %collective-permute-done.23 = bf16[2,96,768]{2,1,0:T(8,128)(2,1)S(1)} collective-permute-done((bf16[2,96,768]{2,1,0:T(8,128)(2,1)S(1)}, bf16[2,96,768]{2,1,0:T(8,128)(2,1)S(1)}, u32[]{:S(2)}, u32[]{:S(2)}) %collective-permute-start.23) | collective-permute-done | bytes 294944 | tf_op jit(solution)/shard_map/ppermute | solution.py:436
  391.9 2.1 collective-permute-start.24
  394.0 2.3 collective-permute-done.19
  397.1 2.5 collective-permute-done.24
  (149 shorter events, 27.1 us)
Async XLA Ops:
  7.2 122.5 %copy-start = (bf16[1,1024,768]{2,1,0:T(8,128)(2,1)S(1)}, bf16[1,1024,768]{2,1,0:T(8,128)(2,1)}, u32[]{:S(2)}) copy-start(bf16[1,1024,768]{2,1,0:T(8,128)(2,1)} %param.15) | copy-start | bytes 4718596
  7.2 118.4 %all-gather.2.cloned.1.call-start = ((), (), s32[]{:S(2)}) async-start(), calls=%async_computation | async-start | bytes 14800896 | tf_op jit(solution)/shard_map/all_gather | solution.py:489
  136.9 2.1 copy-start.18
  139.1 1.2 copy-start.21
  168.1 36.5 %copy-start.24 = (bf16[12,256,256]{2,1,0:T(8,128)(2,1)}, bf16[12,256,256]{2,1,0:T(8,128)(2,1)S(1)}, u32[]{:S(2)}) copy-start(bf16[12,256,256]{2,1,0:T(8,128)(2,1)S(1)} %get-tuple-element.69.rest_4_) | copy-start | bytes 4718596
  168.1 36.6 %copy-start.6 = (bf16[1024,768]{1,0:T(8,128)(2,1)S(1)}, bf16[1024,768]{1,0:T(8,128)(2,1)}, u32[]{:S(2)}) copy-start(bf16[1024,768]{1,0:T(8,128)(2,1)} %copy-done.5) | copy-start | bytes 4718596
  204.7 1.4 copy-start.25
  206.1 20.8 %copy-start.1 = (bf16[1,1024,768]{2,1,0:T(8,128)(2,1)S(1)}, bf16[1,1024,768]{2,1,0:T(8,128)(2,1)}, u32[]{:S(2)}) copy-start(bf16[1,1024,768]{2,1,0:T(8,128)(2,1)} %param.15) | copy-start | bytes 4718596
  206.1 20.8 %copy-start.4 = (f32[1024,768]{1,0:T(8,128)S(1)}, f32[1024,768]{1,0:T(8,128)}, u32[]{:S(2)}) copy-start(f32[1024,768]{1,0:T(8,128)} %get-tuple-element.62.dr_ref) | copy-start | bytes 9437188
  226.9 2.3 copy-start.2
  229.2 9.0 %copy-start.8 = (f32[1,3072]{1,0:T(1,128)S(1)}, f32[1,3072]{1,0:T(1,128)}, u32[]{:S(2)}) copy-start(f32[1,3072]{1,0:T(1,128)} %get-tuple-element.81.refs_7_) | copy-start | bytes 36868
  229.2 9.0 %copy-start.9 = (f32[1,768]{1,0:T(1,128)S(1)}, f32[1,768]{1,0:T(1,128)}, u32[]{:S(2)}) copy-start(f32[1,768]{1,0:T(1,128)} %get-tuple-element.79.refs_5_) | copy-start | bytes 9220
  229.2 9.0 %copy-start.10 = (f32[1,768]{1,0:T(1,128)S(1)}, f32[1,768]{1,0:T(1,128)}, u32[]{:S(2)}) copy-start(f32[1,768]{1,0:T(1,128)} %get-tuple-element.77.refs_3_) | copy-start | bytes 9220
  229.3 9.0 %copy-start.11 = (f32[1,768]{1,0:T(1,128)S(1)}, f32[1,768]{1,0:T(1,128)}, u32[]{:S(2)}) copy-start(f32[1,768]{1,0:T(1,128)} %get-tuple-element.78.refs_4_) | copy-start | bytes 9220
  229.3 9.0 %copy-start.12 = (f32[1,768]{1,0:T(1,128)S(1)}, f32[1,768]{1,0:T(1,128)}, u32[]{:S(2)}) copy-start(f32[1,768]{1,0:T(1,128)} %get-tuple-element.76.refs_2_) | copy-start | bytes 9220
  229.3 9.5 %copy-start.3 = (bf16[3,1024,768]{2,1,0:T(8,128)(2,1)S(1)}, bf16[3,1024,768]{2,1,0:T(8,128)(2,1)}, u32[]{:S(2)}) copy-start(bf16[3,1024,768]{2,1,0:T(8,128)(2,1)} %shard_map.258.dq_ref.b_ref) | copy-start | bytes 14155780
  229.3 9.5 %copy-start.22 = (bf16[1024,768]{1,0:T(8,128)(2,1)S(1)}, bf16[1024,768]{1,0:T(8,128)(2,1)}, u32[]{:S(2)}) copy-start(bf16[1024,768]{1,0:T(8,128)(2,1)} %copy-done.21) | copy-start | bytes 4718596
  238.7 9.1 %collective-permute-start = (f32[2,2,2,2,8,128]{5,4,3,2,0,1:T(8,128)S(1)}, f32[2,2,2,2,8,128]{5,4,3,2,0,1:T(8,128)S(1)}, u32[]{:S(2)}, u32[]{:S(2)}) collective-permute-start(f32[2,2,2,2,8,128]{5,4,3,2,0,1:T(8,128)S(1)} %bitcast.183), channel_id=1, source_target_pairs={{0,1},{1,0},{2,3},{3,2},{4,5},{5,4},{6,7},{7,6},{8,9},{9,8},{10,11... | collective-permute-start | bytes 196616 | tf_op jit(solution)/shard_map/ppermute | solution.py:436
  243.8 2.0 copy-start.23
  245.2 57.5 %collective-permute-start.5 = (bf16[2,2,2,2,24,2304]{5,4,2,3,0,1:T(8,128)(2,1)}, bf16[2,2,2,2,24,2304]{5,4,2,3,0,1:T(8,128)(2,1)}, u32[]{:S(2)}, u32[]{:S(2)}) collective-permute-start(bf16[2,2,2,2,24,2304]{5,4,2,3,0,1:T(8,128)(2,1)} %bitcast.166), channel_id=1, source_target_pairs={{0,1},{1,0},{2,3},{3,2},{4,5},{5,4},{6,7},{7,6},{8,9},{9,8},{10,11... | collective-permute-start | bytes 5308424 | tf_op jit(solution)/shard_map/ppermute | solution.py:436
  245.8 3.4 copy-start.20
  247.3 34.1 %slice-start = ((s8[6291456]{0:T(1024)(128)(4,1)}), s8[4194304]{0:T(1024)(128)(4,1)S(1)}, s32[]{:S(2)}) async-start(s8[6291456]{0:T(1024)(128)(4,1)} %bitcast.177), calls=%async_computation.1 | async-start | bytes 8388608
  247.4 40.8 %collective-permute-start.10 = (bf16[2,2,2,2,24,768]{5,4,2,3,0,1:T(8,128)(2,1)S(1)}, bf16[2,2,2,2,24,768]{5,4,2,3,0,1:T(8,128)(2,1)S(1)}, u32[]{:S(2)}, u32[]{:S(2)}) collective-permute-start(bf16[2,2,2,2,24,768]{5,4,2,3,0,1:T(8,128)(2,1)S(1)} %bitcast.182), channel_id=1, source_target_pairs={{0,1},{1,0},{2,3},{3,2},{4,5},{5,4},{6,7},{7,6},{8,9},{9,8},{10,11... | collective-permute-start | bytes 1769480 | tf_op jit(solution)/shard_map/ppermute | solution.py:436
  247.8 10.7 %collective-permute-start.1 = (f32[2,2,2,8,128]{4,3,2,1,0:T(8,128)S(1)}, f32[2,2,2,8,128]{4,3,2,1,0:T(8,128)S(1)}, u32[]{:S(2)}, u32[]{:S(2)}) collective-permute-start(f32[2,2,2,8,128]{4,3,2,1,0:T(8,128)S(1)} %dynamic-slice_bitcast_fusion.16), channel_id=1, source_target_pairs={{0,8},{1,9},{2,10},{3,11},{4,12},{5,13},{6,14},{7,15},{8,0},{9,1},... | collective-permute-start | bytes 98312 | tf_op jit(solution)/shard_map/ppermute | solution.py:436
  249.3 2.8 copy-start.17
  252.0 29.3 %slice-start.1 = ((s8[6291456]{0:T(1024)(128)(4,1)}), s8[2097152]{0:T(1024)(128)(4,1)S(1)}, s32[]{:S(2)}) async-start(s8[6291456]{0:T(1024)(128)(4,1)} %bitcast.177), calls=%async_computation.2 | async-start | bytes 4194304
  258.6 20.8 %collective-permute-start.2 = (f32[2,2,8,128]{3,2,1,0:T(8,128)S(1)}, f32[2,2,8,128]{3,2,1,0:T(8,128)S(1)}, u32[]{:S(2)}, u32[]{:S(2)}) collective-permute-start(f32[2,2,8,128]{3,2,1,0:T(8,128)S(1)} %dynamic-slice_bitcast_fusion.17), channel_id=1, source_target_pairs={{0,16},{1,17},{2,18},{3,19},{4,20},{5,21},{6,22},{7,23},{8,24},{9,... | collective-permute-start | bytes 49160 | tf_op jit(solution)/shard_map/ppermute | solution.py:436
  277.9 3.4 copy-start.19
  278.1 46.5 %collective-permute-start.15 = (bf16[2,2,2,2,24,3072]{5,4,2,3,0,1:T(8,128)(2,1)S(1)}, bf16[2,2,2,2,24,3072]{5,4,2,3,0,1:T(8,128)(2,1)S(1)}, u32[]{:S(2)}, u32[]{:S(2)}) collective-permute-start(bf16[2,2,2,2,24,3072]{5,4,2,3,0,1:T(8,128)(2,1)S(1)} %bitcast.179), channel_id=1, source_target_pairs={{0,1},{1,0},{2,3},{3,2},{4,5},{5,4},{6,7},{7,6},{8,9},{9,8},{10,11... | collective-permute-start | bytes 7077896 | tf_op jit(solution)/shard_map/ppermute | solution.py:436
  279.3 8.5 %collective-permute-start.3 = (f32[2,8,128]{2,1,0:T(8,128)S(1)}, f32[2,8,128]{2,1,0:T(8,128)S(1)}, u32[]{:S(2)}, u32[]{:S(2)}) collective-permute-start(f32[2,8,128]{2,1,0:T(8,128)S(1)} %fusion.18), channel_id=1, source_target_pairs={{0,2},{1,3},{2,0},{3,1},{4,6},{5,7},{6,4},{7,5},{8,10},{9,11},{10,... | collective-permute-start | bytes 24584 | tf_op jit(solution)/shard_map/ppermute | solution.py:436
  287.9 4.6 %collective-permute-start.4 = (f32[8,128]{1,0:T(8,128)S(1)}, f32[8,128]{1,0:T(8,128)S(1)}, u32[]{:S(2)}, u32[]{:S(2)}) collective-permute-start(f32[8,128]{1,0:T(8,128)S(1)} %fusion.21), channel_id=1, source_target_pairs={{0,4},{1,5},{2,6},{3,7},{4,0},{5,1},{6,2},{7,3},{8,12},{9,13},{10,... | collective-permute-start | bytes 12296 | tf_op jit(solution)/shard_map/ppermute | solution.py:436
  288.4 7.6 %collective-permute-start.11 = (bf16[2,2,2,24,768]{4,3,1,2,0:T(8,128)(2,1)S(1)}, bf16[2,2,2,24,768]{4,3,1,2,0:T(8,128)(2,1)S(1)}, u32[]{:S(2)}, u32[]{:S(2)}) collective-permute-start(bf16[2,2,2,24,768]{4,3,1,2,0:T(8,128)(2,1)S(1)} %dynamic-slice_bitcast_fusion.8), channel_id=1, source_target_pairs={{0,8},{1,9},{2,10},{3,11},{4,12},{5,13},{6,14},{7,15},{8,0},{9,1},... | collective-permute-start | bytes 884744 | tf_op jit(solution)/shard_map/ppermute | solution.py:436
  290.7 41.6 %collective-permute-start.20 = (bf16[2,2,2,2,96,768]{5,4,2,3,0,1:T(8,128)(2,1)S(1)}, bf16[2,2,2,2,96,768]{5,4,2,3,0,1:T(8,128)(2,1)S(1)}, u32[]{:S(2)}, u32[]{:S(2)}) collective-permute-start(bf16[2,2,2,2,96,768]{5,4,2,3,0,1:T(8,128)(2,1)S(1)} %bitcast.180), channel_id=1, source_target_pairs={{0,1},{1,0},{2,3},{3,2},{4,5},{5,4},{6,7},{7,6},{8,9},{9,8},{10,11... | collective-permute-start | bytes 7077896 | tf_op jit(solution)/shard_map/ppermute | solution.py:436
  296.1 5.2 %collective-permute-start.12 = (bf16[2,2,24,768]{3,2,0,1:T(8,128)(2,1)S(1)}, bf16[2,2,24,768]{3,2,0,1:T(8,128)(2,1)S(1)}, u32[]{:S(2)}, u32[]{:S(2)}) collective-permute-start(bf16[2,2,24,768]{3,2,0,1:T(8,128)(2,1)S(1)} %dynamic-slice_bitcast_fusion.12), channel_id=1, source_target_pairs={{0,16},{1,17},{2,18},{3,19},{4,20},{5,21},{6,22},{7,23},{8,24},{9,... | collective-permute-start | bytes 442376 | tf_op jit(solution)/shard_map/ppermute | solution.py:436
  301.4 5.5 %collective-permute-start.13 = (bf16[2,24,768]{2,1,0:T(8,128)(2,1)S(1)}, bf16[2,24,768]{2,1,0:T(8,128)(2,1)S(1)}, u32[]{:S(2)}, u32[]{:S(2)}) collective-permute-start(bf16[2,24,768]{2,1,0:T(8,128)(2,1)S(1)} %dynamic-slice_bitcast_fusion.14), channel_id=1, source_target_pairs={{0,2},{1,3},{2,0},{3,1},{4,6},{5,7},{6,4},{7,5},{8,10},{9,11},{10,... | collective-permute-start | bytes 221192 | tf_op jit(solution)/shard_map/ppermute | solution.py:436
  304.7 18.2 %collective-permute-start.6 = (bf16[2,2,2,24,2304]{4,3,1,2,0:T(8,128)(2,1)S(1)}, bf16[2,2,2,24,2304]{4,3,1,2,0:T(8,128)(2,1)S(1)}, u32[]{:S(2)}, u32[]{:S(2)}) collective-permute-start(bf16[2,2,2,24,2304]{4,3,1,2,0:T(8,128)(2,1)S(1)} %dynamic-slice_bitcast_fusion.2), channel_id=1, source_target_pairs={{0,8},{1,9},{2,10},{3,11},{4,12},{5,13},{6,14},{7,15},{8,0},{9,1},... | collective-permute-start | bytes 2654216 | tf_op jit(solution)/shard_map/ppermute | solution.py:436
  307.0 5.3 %collective-permute-start.14 = (bf16[24,768]{1,0:T(8,128)(2,1)S(1)}, bf16[24,768]{1,0:T(8,128)(2,1)S(1)}, u32[]{:S(2)}, u32[]{:S(2)}) collective-permute-start(bf16[24,768]{1,0:T(8,128)(2,1)S(1)} %dynamic-slice_bitcast_fusion.15), channel_id=1, source_target_pairs={{0,4},{1,5},{2,6},{3,7},{4,0},{5,1},{6,2},{7,3},{8,12},{9,13},{10,... | collective-permute-start | bytes 110600 | tf_op jit(solution)/shard_map/ppermute | solution.py:436
  323.1 8.4 %collective-permute-start.7 = (bf16[2,2,24,2304]{3,2,0,1:T(8,128)(2,1)S(1)}, bf16[2,2,24,2304]{3,2,0,1:T(8,128)(2,1)S(1)}, u32[]{:S(2)}, u32[]{:S(2)}) collective-permute-start(bf16[2,2,24,2304]{3,2,0,1:T(8,128)(2,1)S(1)} %dynamic-slice_bitcast_fusion.5), channel_id=1, source_target_pairs={{0,16},{1,17},{2,18},{3,19},{4,20},{5,21},{6,22},{7,23},{8,24},{9,... | collective-permute-start | bytes 1327112 | tf_op jit(solution)/shard_map/ppermute | solution.py:436
  325.6 29.0 %collective-permute-start.16 = (bf16[2,2,2,24,3072]{4,3,1,2,0:T(8,128)(2,1)S(1)}, bf16[2,2,2,24,3072]{4,3,1,2,0:T(8,128)(2,1)S(1)}, u32[]{:S(2)}, u32[]{:S(2)}) collective-permute-start(bf16[2,2,2,24,3072]{4,3,1,2,0:T(8,128)(2,1)S(1)} %dynamic-slice_bitcast_fusion.1), channel_id=1, source_target_pairs={{0,8},{1,9},{2,10},{3,11},{4,12},{5,13},{6,14},{7,15},{8,0},{9,1},... | collective-permute-start | bytes 3538952 | tf_op jit(solution)/shard_map/ppermute | solution.py:436
  331.6 7.2 %collective-permute-start.8 = (bf16[2,24,2304]{2,1,0:T(8,128)(2,1)S(1)}, bf16[2,24,2304]{2,1,0:T(8,128)(2,1)S(1)}, u32[]{:S(2)}, u32[]{:S(2)}) collective-permute-start(bf16[2,24,2304]{2,1,0:T(8,128)(2,1)S(1)} %dynamic-slice_bitcast_fusion.9), channel_id=1, source_target_pairs={{0,2},{1,3},{2,0},{3,1},{4,6},{5,7},{6,4},{7,5},{8,10},{9,11},{10,... | collective-permute-start | bytes 663560 | tf_op jit(solution)/shard_map/ppermute | solution.py:436
  333.1 40.7 %collective-permute-start.21 = (bf16[2,2,2,96,768]{4,3,1,2,0:T(8,128)(2,1)S(1)}, bf16[2,2,2,96,768]{4,3,1,2,0:T(8,128)(2,1)S(1)}, u32[]{:S(2)}, u32[]{:S(2)}) collective-permute-start(bf16[2,2,2,96,768]{4,3,1,2,0:T(8,128)(2,1)S(1)} %dynamic-slice_bitcast_fusion), channel_id=1, source_target_pairs={{0,8},{1,9},{2,10},{3,11},{4,12},{5,13},{6,14},{7,15},{8,0},{9,1},... | collective-permute-start | bytes 3538952 | tf_op jit(solution)/shard_map/ppermute | solution.py:436
  338.9 16.9 %collective-permute-start.9 = (bf16[24,2304]{1,0:T(8,128)(2,1)S(1)}, bf16[24,2304]{1,0:T(8,128)(2,1)S(1)}, u32[]{:S(2)}, u32[]{:S(2)}) collective-permute-start(bf16[24,2304]{1,0:T(8,128)(2,1)S(1)} %dynamic-slice_bitcast_fusion.13), channel_id=1, source_target_pairs={{0,4},{1,5},{2,6},{3,7},{4,0},{5,1},{6,2},{7,3},{8,12},{9,13},{10,... | collective-permute-start | bytes 331784 | tf_op jit(solution)/shard_map/ppermute | solution.py:436
  355.0 20.2 %collective-permute-start.17 = (bf16[2,2,24,3072]{3,2,0,1:T(8,128)(2,1)S(1)}, bf16[2,2,24,3072]{3,2,0,1:T(8,128)(2,1)S(1)}, u32[]{:S(2)}, u32[]{:S(2)}) collective-permute-start(bf16[2,2,24,3072]{3,2,0,1:T(8,128)(2,1)S(1)} %dynamic-slice_bitcast_fusion.4), channel_id=1, source_target_pairs={{0,16},{1,17},{2,18},{3,19},{4,20},{5,21},{6,22},{7,23},{8,24},{9,... | collective-permute-start | bytes 1769480 | tf_op jit(solution)/shard_map/ppermute | solution.py:436
  374.2 9.9 %collective-permute-start.22 = (bf16[2,2,96,768]{3,2,0,1:T(8,128)(2,1)S(1)}, bf16[2,2,96,768]{3,2,0,1:T(8,128)(2,1)S(1)}, u32[]{:S(2)}, u32[]{:S(2)}) collective-permute-start(bf16[2,2,96,768]{3,2,0,1:T(8,128)(2,1)S(1)} %dynamic-slice_bitcast_fusion.3), channel_id=1, source_target_pairs={{0,16},{1,17},{2,18},{3,19},{4,20},{5,21},{6,22},{7,23},{8,24},{9,... | collective-permute-start | bytes 1769480 | tf_op jit(solution)/shard_map/ppermute | solution.py:436
  375.4 10.6 %collective-permute-start.18 = (bf16[2,24,3072]{2,1,0:T(8,128)(2,1)S(1)}, bf16[2,24,3072]{2,1,0:T(8,128)(2,1)S(1)}, u32[]{:S(2)}, u32[]{:S(2)}) collective-permute-start(bf16[2,24,3072]{2,1,0:T(8,128)(2,1)S(1)} %dynamic-slice_bitcast_fusion.7), channel_id=1, source_target_pairs={{0,2},{1,3},{2,0},{3,1},{4,6},{5,7},{6,4},{7,5},{8,10},{9,11},{10,... | collective-permute-start | bytes 884744 | tf_op jit(solution)/shard_map/ppermute | solution.py:436
  384.3 7.5 %collective-permute-start.23 = (bf16[2,96,768]{2,1,0:T(8,128)(2,1)S(1)}, bf16[2,96,768]{2,1,0:T(8,128)(2,1)S(1)}, u32[]{:S(2)}, u32[]{:S(2)}) collective-permute-start(bf16[2,96,768]{2,1,0:T(8,128)(2,1)S(1)} %dynamic-slice_bitcast_fusion.6), channel_id=1, source_target_pairs={{0,2},{1,3},{2,0},{3,1},{4,6},{5,7},{6,4},{7,5},{8,10},{9,11},{10,... | collective-permute-start | bytes 884744 | tf_op jit(solution)/shard_map/ppermute | solution.py:436
  386.1 10.2 %collective-permute-start.19 = (bf16[24,3072]{1,0:T(8,128)(2,1)S(1)}, bf16[24,3072]{1,0:T(8,128)(2,1)S(1)}, u32[]{:S(2)}, u32[]{:S(2)}) collective-permute-start(bf16[24,3072]{1,0:T(8,128)(2,1)S(1)} %dynamic-slice_bitcast_fusion.11), channel_id=1, source_target_pairs={{0,4},{1,5},{2,6},{3,7},{4,0},{5,1},{6,2},{7,3},{8,12},{9,13},{10,... | collective-permute-start | bytes 442376 | tf_op jit(solution)/shard_map/ppermute | solution.py:436
  391.9 7.7 %collective-permute-start.24 = (bf16[96,768]{1,0:T(8,128)(2,1)S(1)}, bf16[96,768]{1,0:T(8,128)(2,1)S(1)}, u32[]{:S(2)}, u32[]{:S(2)}) collective-permute-start(bf16[96,768]{1,0:T(8,128)(2,1)S(1)} %dynamic-slice_bitcast_fusion.10), channel_id=1, source_target_pairs={{0,4},{1,5},{2,6},{3,7},{4,0},{5,1},{6,2},{7,3},{8,12},{9,13},{10,... | collective-permute-start | bytes 442376 | tf_op jit(solution)/shard_map/ppermute | solution.py:436
  (7 other events, 4.8 us)
Sparse Core Ops, SparseCore 0:
  18.8 106.7 all-gather.1
